TPU v7x, 256 devices: a whole 4x4x8 slice. The times are simulated.
256 devices in a mesh: node: 64 (over y, z_hi, x, core), local: 4 (over z_lo).
Axes of the slice: x: 4, y: 4, z: 8 (z_hi: 2, z_lo: 4; z = z_hi * 4 + z_lo), core: 2. Of those that a mesh axis runs over, the one named last changes fastest.
Arguments:
- tokens: bfloat16 [65536, 4096], P(('node', 'local')), may hold values from -24 to 24
- queries: bfloat16 [65536, 4096], P(('node', 'local')), may hold values from -240 to 240
- values: bfloat16 [65536, 512], P(('node', 'local')), may hold values from -6 to 6
- upstream: bfloat16 [65536, 4096], P(('node', 'local')), may hold values from -6 to 6
- key_weight: bfloat16 [4096, 512], P(('node', 'local')), may hold values from -0.09375 to 0.09375
- positions: int32 [65536], P(('node', 'local')), may hold values from 0 to 255, as said below
Outputs:
- grad_tokens: bfloat16 [65536, 4096], P(('node', 'local'))
- grad_weight: float32 [4096, 512], P(('node', 'local'))
Inputs may be any that keep to these rules, and one draw needn't show every extreme that they name: positions[i] counts the earlier tokens of token i's document; every block of 256 rows starts a document, and no document crosses such a block.
All inputs are finite; a program needn't handle non-finite values.
Results may differ from a plain program's by a relative error of at most 0.033.
Values may be sent and summed in bfloat16 or wider, within the bound.
A program may use at most 128 MiB of HBM per device.

v0:
```python
import jax
import jax.numpy as jnp
from jax import lax
from jax.sharding import Mesh
from jax.sharding import PartitionSpec as P

HEAD_SIZE = 128
NODE = ("node_0", "node_1", "node_2", "node_3")
NODE_LOCAL = ("node_0", "node_1", "node_2", "node_3", "local")


def piece_ends(length, count):
    unit = 8 if length >= 8 * count else 1
    return [length // unit * k // count * unit for k in range(1, count)]


def stacked_from(shard, axes, sequence):
    tiles = shard
    for k in sequence:
        tiles = lax.all_gather(tiles, axes[k])
    done = sequence[::-1]
    back = [done.index(k) for k in range(len(axes))]
    tiles = tiles.transpose(*back, *range(len(axes), tiles.ndim))
    return tiles.reshape(-1, *shard.shape)


def in_order(tiles, dim):
    tiles = jnp.moveaxis(tiles, 0, dim)
    dims = tiles.shape
    return tiles.reshape(*dims[:dim], dims[dim] * dims[dim + 1], *dims[dim + 2 :])


def gather_at_once(shard, axes, dim):
    numbers = list(range(len(axes)))[::-1]
    widest = shard.shape.index(max(shard.shape[:-1] or shard.shape))
    edges = [0, *piece_ends(shard.shape[widest], len(axes)), shard.shape[widest]]
    outs = []
    for k, (start, end) in enumerate(zip(edges, edges[1:])):
        if end > start:
            section = lax.slice_in_dim(shard, start, end, axis=widest)
            outs.append(stacked_from(section, axes, numbers[k:] + numbers[:k]))
    return in_order(jnp.concatenate(outs, axis=widest + 1), dim)


def cut_along(shard, dim, size):
    dims = shard.shape
    tiles = shard.reshape(*dims[:dim], size, dims[dim] // size, *dims[dim + 1 :])
    return jnp.moveaxis(tiles, dim, 0)


def sent_and_summed(shard, axis, dim):
    tiles = cut_along(shard, dim, lax.axis_size(axis))
    arrived = lax.all_to_all(tiles, axis, split_axis=0, concat_axis=0, tiled=True)
    return arrived.sum(axis=0)


def angle_tables(positions, head_width):
    half = head_width // 2
    freq = jnp.exp(
        -(jnp.arange(half, dtype=jnp.float32) * 2.0 / head_width) * jnp.log(jnp.float32(1000000.0))
    )
    angle = positions.astype(jnp.float32)[:, None] * freq[None, :]
    return (jnp.cos(angle)[:, None, :], jnp.sin(angle)[:, None, :])


def rotate(raw_keys, cosine, sine_part, head_width, sign):
    item_count, width = raw_keys.shape
    shaped = raw_keys.reshape(item_count, width // head_width, head_width)
    half = head_width // 2
    first, second = (shaped[..., :half], shaped[..., half:])
    joined = jnp.concatenate(
        [first * cosine - sign * second * sine_part, second * cosine + sign * first * sine_part],
        axis=-1,
    )
    return joined.reshape(item_count, width)


def attend_back(queries, keys, values, upstream, positions, head_width):
    item_count, width = keys.shape
    key_value_count = width // head_width
    group_size = queries.shape[1] // width
    scale = head_width ** (-0.5)
    qmat = queries.reshape(item_count, key_value_count, group_size, head_width)
    kmat = keys.reshape(item_count, key_value_count, head_width)
    value_matrix = values.reshape(item_count, key_value_count, head_width)
    upper_matrix = upstream.reshape(item_count, key_value_count, group_size, head_width)
    scores = jnp.einsum("yxru,oxu->xryo", qmat, kmat, preferred_element_type=jnp.float32) * scale
    place = jnp.arange(item_count, dtype=jnp.int32)
    allowed = (place[None, :] <= place[:, None]) & (place[None, :] >= (place - positions)[:, None])
    scores = jnp.where(allowed, scores, jnp.float32(-1e30))
    top = jnp.max(scores, axis=-1, keepdims=True)
    expo = jnp.exp(scores - top)
    probs = expo / jnp.sum(expo, axis=-1, keepdims=True)
    slope_values = jnp.einsum(
        "yxru,oxu->xryo", upper_matrix, value_matrix, preferred_element_type=jnp.float32
    )
    inner = jnp.sum(probs * slope_values, axis=-1, keepdims=True)
    dscores = (probs * (slope_values - inner) * scale).astype(jnp.bfloat16)
    grad_rot = jnp.einsum("kgts,tkgd->skd", dscores, qmat, preferred_element_type=jnp.float32)
    return grad_rot.reshape(item_count, width)


def per_device(tokens, queries, values, upstream, key_weight, positions):
    node_count = lax.axis_size(NODE)
    local_count = lax.axis_size("local")
    local_index = lax.axis_index("local")
    shard_rows = key_weight.shape[0]
    key_width = key_weight.shape[1]
    item_count = tokens.shape[0]
    model_width = tokens.shape[1]
    head_width = HEAD_SIZE
    whole_weight = gather_at_once(key_weight, NODE_LOCAL, 0)
    raw_keys = jnp.dot(tokens, whole_weight, preferred_element_type=jnp.float32)
    grouped = whole_weight.reshape(node_count, local_count, shard_rows, key_width)
    quarter = lax.dynamic_index_in_dim(grouped, local_index, 1, keepdims=False)
    quarter = quarter.reshape(node_count * shard_rows, key_width)
    cosine, sine_part = angle_tables(positions, head_width)
    keys = rotate(raw_keys, cosine, sine_part, head_width, 1.0).astype(jnp.bfloat16)
    grad_rot = attend_back(queries, keys, values, upstream, positions, head_width)
    grad_keys = rotate(grad_rot, cosine, sine_part, head_width, -1.0).astype(jnp.bfloat16)
    mixed = lax.dot_general(
        grad_keys,
        lax.all_gather(quarter, "local", axis=0, tiled=True),
        (((1,), (1,)), ((), ())),
        preferred_element_type=jnp.float32,
    ).astype(jnp.bfloat16)
    grad_tokens = mixed.reshape(item_count, local_count, node_count, shard_rows)
    grad_tokens = jnp.transpose(grad_tokens, (0, 2, 1, 3)).reshape(item_count, model_width)
    sectioned = lax.psum_scatter(
        lax.dot_general(
            tokens, grad_keys, (((0,), (0,)), ((), ())), preferred_element_type=jnp.float32
        ),
        NODE,
        scatter_dimension=0,
        tiled=True,
    )
    grad_weight = sent_and_summed(sectioned, "local", 0)
    return (grad_tokens, grad_weight)


def solution(mesh):
    torus = Mesh(
        mesh.devices.reshape(4, 2, 4, 2, mesh.shape["local"]),
        ("node_0", "node_1", "node_2", "node_3", "local"),
    )
    placed = (
        P(NODE_LOCAL, None),
        P(NODE_LOCAL, None),
        P(NODE_LOCAL, None),
        P(NODE_LOCAL, None),
        P(NODE_LOCAL, None),
        P(NODE_LOCAL),
    )
    return jax.shard_map(
        per_device,
        mesh=torus,
        in_specs=placed,
        out_specs=(P(NODE_LOCAL, None), P(NODE_LOCAL, None)),
        check_vma=False,
    )
```

profile of v0, /device:TPU:1, one launch (start us, length us, event | category | flops | bytes accessed | tf_op | source)
XLA Modules:
  0.0 926.5 jit_solution(6340969713008578064)
XLA Ops:
  7.2 0.8 slice_bitcast_fusion
  8.1 10.4 %all-gather.29 = bf16[4,4,512]{2,1,0:T(4,128)(2,1)S(1)} all-gather(bf16[1,4,512]{2,1,0:T(4,128)(2,1)S(1)} %slice_bitcast_fusion), channel_id=22, replica_groups=mesh['node_0'=4,'node_1'=2,'node_2'=4,'node_3'=2,'local'=4] {'node_0'}, dimensions={0}, use_global_device_ids=true | all-gather | bytes 20480 | tf_op jit(solution)/shard_map/all_gather | solution.py:20
  18.4 11.4 %all-gather.21 = bf16[16,4,512]{2,1,0:T(4,128)(2,1)S(1)} all-gather(bf16[4,4,512]{2,1,0:T(4,128)(2,1)S(1)} %all-gather.29), channel_id=23, replica_groups=mesh['node_0'=4,'node_1'=2,'node_2'=4,'node_3'=2,'local'=4] {'local'}, dimensions={0}, use_global_device_ids=true | all-gather | bytes 81920 | tf_op jit(solution)/shard_map/all_gather | solution.py:20
  29.9 8.1 all-gather.22
  38.0 10.9 %all-gather.23 = bf16[8,4,4,4,512]{4,3,2,1,0:T(4,128)(2,1)} all-gather(bf16[2,4,4,4,512]{4,3,2,1,0:T(4,128)(2,1)S(1)} %bitcast.150), channel_id=25, replica_groups=mesh['node_0'=4,'node_1'=2,'node_2'=4,'node_3'=2,'local'=4] {'node_2'}, dimensions={0}, use_global_device_ids=true | all-gather | bytes 655360 | tf_op jit(solution)/shard_map/all_gather | solution.py:20
  49.0 0.8 slice_bitcast_fusion.1
  49.8 4.4 all-gather.26
  54.3 9.0 all-gather.6
  63.3 7.9 all-gather.7
  71.3 10.6 %all-gather.8 = bf16[8,4,2,3,512]{4,1,3,2,0:T(4,128)(2,1)S(1)} all-gather(bf16[2,4,2,3,512]{4,1,3,2,0:T(4,128)(2,1)S(1)} %copy.136), channel_id=10, replica_groups=mesh['node_0'=4,'node_1'=2,'node_2'=4,'node_3'=2,'local'=4] {'node_0'}, dimensions={0}, use_global_device_ids=true | all-gather | bytes 245760 | tf_op jit(solution)/shard_map/all_gather | solution.py:20
  81.9 21.4 %all-gather.9 = bf16[16,2,4,2,3,512]{5,2,4,3,1,0:T(4,128)(2,1)S(1)} all-gather(bf16[4,2,4,2,3,512]{5,2,4,3,1,0:T(4,128)(2,1)S(1)} %bitcast.149), channel_id=11, replica_groups=mesh['node_0'=4,'node_1'=2,'node_2'=4,'node_3'=2,'local'=4] {'local'}, dimensions={0}, use_global_device_ids=true | all-gather | bytes 983040 | tf_op jit(solution)/shard_map/all_gather | solution.py:20
  103.3 0.8 copy.137
  104.6 9.6 %all-gather.27 = bf16[4,3,512]{2,1,0:T(4,128)(2,1)S(1)} all-gather(bf16[1,3,512]{2,1,0:T(4,128)(2,1)S(1)} %get-tuple-element.19), channel_id=12, replica_groups=mesh['node_0'=4,'node_1'=2,'node_2'=4,'node_3'=2,'local'=4] {'node_2'}, dimensions={0}, use_global_device_ids=true | all-gather | bytes 15360 | tf_op jit(solution)/shard_map/all_gather | solution.py:20
  114.2 7.2 all-gather.11
  121.4 9.3 %all-gather.12 = bf16[8,4,3,512]{3,1,2,0:T(4,128)(2,1)S(1)} all-gather(bf16[2,4,3,512]{3,1,2,0:T(4,128)(2,1)S(1)} %copy.139), channel_id=14, replica_groups=mesh['node_0'=4,'node_1'=2,'node_2'=4,'node_3'=2,'local'=4] {'node_0'}, dimensions={0}, use_global_device_ids=true | all-gather | bytes 122880 | tf_op jit(solution)/shard_map/all_gather | solution.py:20
  130.7 11.4 %all-gather.13 = bf16[16,2,4,3,512]{4,2,3,1,0:T(4,128)(2,1)S(1)} all-gather(bf16[4,2,4,3,512]{4,2,3,1,0:T(4,128)(2,1)S(1)} %bitcast.154), channel_id=15, replica_groups=mesh['node_0'=4,'node_1'=2,'node_2'=4,'node_3'=2,'local'=4] {'local'}, dimensions={0}, use_global_device_ids=true | all-gather | bytes 491520 | tf_op jit(solution)/shard_map/all_gather | solution.py:20
  142.2 16.9 %all-gather.14 = bf16[8,4,2,4,3,512]{5,3,4,2,1,0:T(4,128)(2,1)S(1)} all-gather(bf16[4,4,2,4,3,512]{5,3,4,2,1,0:T(4,128)(2,1)S(1)} %bitcast.145), channel_id=16, replica_groups=mesh['node_0'=4,'node_1'=2,'node_2'=4,'node_3'=2,'local'=4] {'node_3'}, dimensions={0}, use_global_device_ids=true | all-gather | bytes 1179648 | tf_op jit(solution)/shard_map/all_gather | solution.py:20
  159.1 1.6 copy.175
  160.7 7.1 all-gather.28
  167.8 9.0 all-gather.16
  176.8 10.3 %all-gather.17 = bf16[16,2,3,512]{3,1,2,0:T(2,128)(2,1)S(1)} all-gather(bf16[4,2,3,512]{3,1,2,0:T(2,128)(2,1)S(1)} %copy.141), channel_id=19, replica_groups=mesh['node_0'=4,'node_1'=2,'node_2'=4,'node_3'=2,'local'=4] {'local'}, dimensions={0}, use_global_device_ids=true | all-gather | bytes 122880 | tf_op jit(solution)/shard_map/all_gather | solution.py:20
  187.2 8.9 all-gather.18
  196.1 12.4 %all-gather.19 = bf16[8,4,4,2,3,512]{5,2,4,3,1,0:T(4,128)(2,1)S(1)} all-gather(bf16[2,4,4,2,3,512]{5,2,4,3,1,0:T(4,128)(2,1)S(1)} %bitcast.147), channel_id=21, replica_groups=mesh['node_0'=4,'node_1'=2,'node_2'=4,'node_3'=2,'local'=4] {'node_2'}, dimensions={0}, use_global_device_ids=true | all-gather | bytes 983040 | tf_op jit(solution)/shard_map/all_gather | solution.py:20
  208.4 0.9 copy-done.2
  209.3 1.6 copy.178
  210.9 10.2 %all-gather.25 = bf16[4,3,512]{2,1,0:T(4,128)(2,1)S(1)} all-gather(bf16[1,3,512]{2,1,0:T(4,128)(2,1)S(1)} %get-tuple-element.21), channel_id=2, replica_groups=mesh['node_0'=4,'node_1'=2,'node_2'=4,'node_3'=2,'local'=4] {'local'}, dimensions={0}, use_global_device_ids=true | all-gather | bytes 15360 | tf_op jit(solution)/shard_map/all_gather | solution.py:20
  221.1 6.3 all-gather.1
  227.5 9.8 %all-gather.2 = bf16[8,4,3,512]{3,1,2,0:T(4,128)(2,1)S(1)} all-gather(bf16[2,4,3,512]{3,1,2,0:T(4,128)(2,1)S(1)} %copy.133), channel_id=4, replica_groups=mesh['node_0'=4,'node_1'=2,'node_2'=4,'node_3'=2,'local'=4] {'node_2'}, dimensions={0}, use_global_device_ids=true | all-gather | bytes 122880 | tf_op jit(solution)/shard_map/all_gather | solution.py:20
  237.3 9.2 all-gather.3
  246.5 10.8 %all-gather.4 = bf16[8,4,2,4,3,512]{5,3,4,2,1,0:T(4,128)(2,1)S(1)} all-gather(bf16[2,4,2,4,3,512]{5,3,4,2,1,0:T(4,128)(2,1)S(1)} %bitcast.148), channel_id=6, replica_groups=mesh['node_0'=4,'node_1'=2,'node_2'=4,'node_3'=2,'local'=4] {'node_0'}, dimensions={0}, use_global_device_ids=true | all-gather | bytes 983040 | tf_op jit(solution)/shard_map/all_gather | solution.py:20
  257.3 1.7 copy.134
  259.0 4.1 copy.190
  263.1 3.4 copy.191
  266.5 1.0 reshape.125
  268.2 1.3 broadcast_multiply_fusion
  269.5 6.2 fusion.15
  275.7 2.8 copy.147
  278.4 53.9 %concatenate.24 = bf16[256,16,512]{2,1,0:T(8,128)(2,1)} concatenate(bf16[256,3,512]{2,1,0:T(4,128)(2,1)} %bitcast.121, bf16[256,3,512]{2,1,0:T(4,128)(2,1)S(1)} %bitcast.119, bf16[256,3,512]{2,1,0:T(4,128)(2,1)} %bitcast.133, bf16[256,3,512]{2,1,0:T(4,128)(2,1)} %bitcast.134, bf16[256,4,512]{2,1,0:T(4,128)(2,1)} %bitcast.123), dimensions={1} | concatenate | bytes 8388608 | tf_op jit(solution)/shard_map/concatenate | solution.py:42
  332.3 3.5 fusion.31
  335.8 0.8 fusion.30
  336.6 2.0 copy.188
  338.6 1.0 copy.189
  339.6 1.4 subtract_convert_fusion.1
  341.0 6.1 fusion.20
  347.1 12.9 %fusion.13 = f32[4,8,256,256]{2,3,1,0:T(8,128)} fusion(f32[4,256,256,8]{2,1,3,0:T(8,128)} %fusion.20, pred[256,256]{0,1:T(8,128)(4,1)} %fusion.24), kind=kOutput, calls=%fused_computation.18 | output fusion | flops 12599806 | bytes 16842752 | tf_op jit(solution)/shard_map/div | solution.py:93
  360.0 14.2 %fusion.17 = f32[256,4,128]{2,0,1:T(8,128)} fusion(bf16[256,4,8,128]{0,3,2,1:T(8,128)(2,1)} %bitcast.128, f32[4,8,256,256]{2,3,1,0:T(8,128)} %fusion.13, f32[4,256,256,8]{2,1,3,0:T(8,128)} %fusion.15), kind=kOutput, calls=%fused_computation.22 | convolution fusion | flops 547365120 | bytes 19398656 | tf_op jit(solution)/shard_map/kgts,tkgd->skd/dot_general | solution.py:99
  374.2 1.5 subtract_convert_fusion
  375.7 0.9 pad_maximum_fusion
  376.6 1.1 copy.159
  377.7 4.5 convolution_bitcast_fusion
  382.1 9.0 copy.183
  391.5 1.7 copy.162
  393.2 1.5 copy.164
  394.7 1.5 copy.145
  396.3 1.6 copy.165
  397.9 53.9 %concatenate.32 = bf16[64,4,16,512]{3,2,1,0:T(8,128)(2,1)} concatenate(bf16[64,4,3,512]{3,2,1,0:T(4,128)(2,1)} %bitcast.122, bf16[64,4,3,512]{3,2,1,0:T(4,128)(2,1)S(1)} %bitcast.120, bf16[64,4,3,512]{3,2,1,0:T(4,128)(2,1)} %copy.164, bf16[64,4,3,512]{3,2,1,0:T(4,128)(2,1)} %copy.165, bf16[64,4,4,512]{3,2,1,0:T(4,128)(2,1)} %bitcast.124), dimensions={2} | concatenate | bytes 8388608 | tf_op jit(solution)/shard_map/concatenate | solution.py:42
  451.8 2.3 constant_dynamic-slice_fusion
  454.1 362.0 %reduce-scatter.4.cloned.1.call-done = f32[64,512]{1,0:T(8,128)} async-done(((f32[4096,512]{1,0:T(8,128)}), f32[64,512]{1,0:T(8,128)}) %reduce-scatter.4.cloned.1.call-update) | async-done | bytes 131088 | tf_op jit(solution)/shard_map/reduce_scatter | solution.py:129
  816.0 3.3 all-to-all-start
  819.4 83.8 %all-gather.33.cloned.1.call-done = bf16[4096,512]{1,0:T(8,128)(2,1)} async-done(((bf16[1024,512]{1,0:T(8,128)(2,1)}), bf16[4096,512]{1,0:T(8,128)(2,1)}) %all-gather.33.cloned.1.call-update) | async-done | bytes 4194320 | tf_op jit(solution)/shard_map/all_gather | solution.py:123
  903.1 4.8 convolution_convert_fusion
  908.0 4.1 copy.166
  912.0 3.2 copy.167
  915.3 4.1 copy.169
  (26 shorter events, 2.4 us)
Async XLA Ops:
  7.2 325.1 %copy-start = (bf16[256,4096]{1,0:T(8,128)(2,1)S(1)}, bf16[256,4096]{1,0:T(8,128)(2,1)}, u32[]{:S(2)}) copy-start(bf16[256,4096]{1,0:T(8,128)(2,1)} %param.6) | copy-start | bytes 6291460
  7.2 268.5 %all-gather.35.cloned.1.call-start = ((), (), s32[]{:S(2)}) async-start(), calls=%async_computation.3 | async-start | bytes 1572864 | tf_op jit(solution)/shard_map/all_gather | solution.py:20
  49.0 767.1 %reduce-scatter.4.cloned.1.call-start = ((), (), s32[]{:S(2)}) async-start(), calls=%async_computation.4 | async-start | bytes 8519680 | tf_op jit(solution)/shard_map/reduce_scatter | solution.py:129
  159.1 99.9 %copy-start.1 = (bf16[8,4,2,4,3,512]{5,3,4,2,1,0:T(4,128)(2,1)}, bf16[8,4,2,4,3,512]{5,3,4,2,1,0:T(4,128)(2,1)S(1)}, u32[]{:S(2)}) copy-start(bf16[8,4,2,4,3,512]{5,3,4,2,1,0:T(4,128)(2,1)S(1)} %all-gather.14) | copy-start | bytes 2359300
  159.1 99.9 %copy-start.3 = (s32[256]{0:T(256)S(1)}, s32[256]{0:T(256)}, u32[]{:S(2)}) copy-start(s32[256]{0:T(256)} %param.11) | copy-start | bytes 3076
  208.4 0.9 copy-start.2
  391.2 512.0 %all-gather.33.cloned.1.call-start = ((), (), s32[]{:S(2)}) async-start(), calls=%async_computation.2 | async-start | bytes 5242880 | tf_op jit(solution)/shard_map/all_gather | solution.py:123
  816.0 103.3 %all-to-all-start = ((f32[4,16,512]{2,1,0:T(8,128)}), f32[4,16,512]{2,1,0:T(8,128)S(1)}, u32[]{:S(2)}, u32[]{:S(2)}) async-start(f32[4,16,512]{2,1,0:T(8,128)} %bitcast.161), calls=%async_computation | async-start | bytes 262144 | tf_op jit(solution)/shard_map/all_to_all | solution.py:53
Sparse Core Ops, SparseCore 0:
  49.1 42.8 all-gather.34
  391.3 424.6 reduce-scatter.3
  818.4 84.6 all-gather.32
where the time goes:
time: 934 us; the launch traced here: 926 us
  waiting for transfers between devices  446 us (48%)
  blocking collectives  243 us (26%)
  local copies, waits for them, and re-layouts  162 us (17%)
  matrix products  39.3 us (4%)
  other arithmetic  19.2 us (2%)
  between operations  13.9 us (1%)
    reduce_scatter x1, waiting for transfers between devices, per_device(): lax.psum_scatter(lax.dot_general(tokens, grad_keys, (((0,), (0,)), ((), (...  362 us
    all_gather x24, blocking collectives, stacked_from(): tiles = lax.all_gather(tiles, axes[k])  243 us
    concatenate x4, local copies, waits for them, and re-layouts, gather_at_once(): return in_order(jnp.concatenate(outs, axis=widest + 1), dim)  111 us
    all_gather x1, waiting for transfers between devices, per_device(): lax.all_gather(quarter, 'local', axis=0, tiled=True)  83.8 us
    unnamed x15, local copies, waits for them, and re-layouts  22.1 us
  transfers between devices with their start and end apart: 4, of which 2 were waited for; matrix products, arithmetic and copies ran while one was open for 11% of the time, Pallas kernels for 0%

commit v1 on v0

--- a/solution.py
+++ b/solution.py
@@ -120,7 +120,9 @@
     grad_keys = rotate(grad_rot, cosine, sine_part, head_width, -1.0).astype(jnp.bfloat16)
     mixed = lax.dot_general(
         grad_keys,
-        lax.all_gather(quarter, "local", axis=0, tiled=True),
+        jnp.concatenate(
+            lax.all_to_all(jnp.stack([quarter] * lax.axis_size("local")), "local", 0, 0), axis=0
+        ),
         (((1,), (1,)), ((), ())),
         preferred_element_type=jnp.float32,
     ).astype(jnp.bfloat16)

time: 934 us -> 868 us (0.929)
  waiting for transfers between devices: 446 us -> 250 us
  blocking collectives: 243 us -> 361 us
    all_to_all x0 -> x1, blocking collectives: none -> 118 us  [per_device(): lax.all_to_all(jnp.stack([quarter] * lax.axis_size('local')), 'local', 0, 0)]
    reduce_scatter x1, waiting for transfers between devices: 362 us -> 250 us  [per_device(): lax.psum_scatter(lax.dot_general(tokens, grad_keys, (((0,), (0,)), ((), (...]
    all_gather x1 -> x0, waiting for transfers between devices: 83.8 us -> none  [per_device(): lax.all_gather(quarter, 'local', axis=0, tiled=True)]
  transfers between devices with their start and end apart: 4 -> 3, of which waited for: 2 -> 1; matrix products, arithmetic and copies ran while one was open for 11% -> 12% of each run, Pallas kernels for 0% -> 0%
where the time goes in v1:
time: 868 us; the launch traced here: 852 us
  blocking collectives  361 us (42%)
  waiting for transfers between devices  250 us (29%)
  local copies, waits for them, and re-layouts  161 us (19%)
  matrix products  39.3 us (5%)
  other arithmetic  19.2 us (2%)
  between operations  14.2 us (2%)
    reduce_scatter x1, waiting for transfers between devices, per_device(): lax.psum_scatter(lax.dot_general(tokens, grad_keys, (((0,), (0,)), ((), (...  250 us
    all_gather x24, blocking collectives, stacked_from(): tiles = lax.all_gather(tiles, axes[k])  243 us
    all_to_all x1, blocking collectives, per_device(): lax.all_to_all(jnp.stack([quarter] * lax.axis_size('local')), 'local', 0, 0)  118 us
    concatenate x4, local copies, waits for them, and re-layouts, gather_at_once(): return in_order(jnp.concatenate(outs, axis=widest + 1), dim)  111 us
    unnamed x15, local copies, waits for them, and re-layouts  22.1 us
  transfers between devices with their start and end apart: 3, of which 1 were waited for; matrix products, arithmetic and copies ran while one was open for 12% of the time, Pallas kernels for 0%

profile of v1, /device:TPU:1, one launch (start us, length us, event | category | flops | bytes accessed | tf_op | source)
XLA Modules:
  0.0 851.8 jit_solution(6088683768232004462)
XLA Ops:
  7.2 0.8 slice_bitcast_fusion
  8.1 10.4 %all-gather.29 = bf16[4,4,512]{2,1,0:T(4,128)(2,1)S(1)} all-gather(bf16[1,4,512]{2,1,0:T(4,128)(2,1)S(1)} %slice_bitcast_fusion), channel_id=22, replica_groups=mesh['node_0'=4,'node_1'=2,'node_2'=4,'node_3'=2,'local'=4] {'node_0'}, dimensions={0}, use_global_device_ids=true | all-gather | bytes 20480 | tf_op jit(solution)/shard_map/all_gather | solution.py:20
  18.4 11.4 %all-gather.21 = bf16[16,4,512]{2,1,0:T(4,128)(2,1)S(1)} all-gather(bf16[4,4,512]{2,1,0:T(4,128)(2,1)S(1)} %all-gather.29), channel_id=23, replica_groups=mesh['node_0'=4,'node_1'=2,'node_2'=4,'node_3'=2,'local'=4] {'local'}, dimensions={0}, use_global_device_ids=true | all-gather | bytes 81920 | tf_op jit(solution)/shard_map/all_gather | solution.py:20
  29.9 8.1 all-gather.22
  38.0 10.9 %all-gather.23 = bf16[8,4,4,4,512]{4,3,2,1,0:T(4,128)(2,1)} all-gather(bf16[2,4,4,4,512]{4,3,2,1,0:T(4,128)(2,1)S(1)} %bitcast.152), channel_id=25, replica_groups=mesh['node_0'=4,'node_1'=2,'node_2'=4,'node_3'=2,'local'=4] {'node_2'}, dimensions={0}, use_global_device_ids=true | all-gather | bytes 655360 | tf_op jit(solution)/shard_map/all_gather | solution.py:20
  49.0 0.8 slice_bitcast_fusion.1
  49.8 4.4 all-gather.26
  54.3 9.0 %all-gather.6 = bf16[8,3,512]{2,1,0:T(4,128)(2,1)S(1)} all-gather(bf16[2,3,512]{2,1,0:T(4,128)(2,1)S(1)} %all-gather.26), channel_id=8, replica_groups=mesh['node_0'=4,'node_1'=2,'node_2'=4,'node_3'=2,'local'=4] {'node_2'}, dimensions={0}, use_global_device_ids=true | all-gather | bytes 30720 | tf_op jit(solution)/shard_map/all_gather | solution.py:20
  63.3 7.9 all-gather.7
  71.3 10.6 %all-gather.8 = bf16[8,4,2,3,512]{4,1,3,2,0:T(4,128)(2,1)S(1)} all-gather(bf16[2,4,2,3,512]{4,1,3,2,0:T(4,128)(2,1)S(1)} %copy.136), channel_id=10, replica_groups=mesh['node_0'=4,'node_1'=2,'node_2'=4,'node_3'=2,'local'=4] {'node_0'}, dimensions={0}, use_global_device_ids=true | all-gather | bytes 245760 | tf_op jit(solution)/shard_map/all_gather | solution.py:20
  81.9 21.4 %all-gather.9 = bf16[16,2,4,2,3,512]{5,2,4,3,1,0:T(4,128)(2,1)S(1)} all-gather(bf16[4,2,4,2,3,512]{5,2,4,3,1,0:T(4,128)(2,1)S(1)} %bitcast.151), channel_id=11, replica_groups=mesh['node_0'=4,'node_1'=2,'node_2'=4,'node_3'=2,'local'=4] {'local'}, dimensions={0}, use_global_device_ids=true | all-gather | bytes 983040 | tf_op jit(solution)/shard_map/all_gather | solution.py:20
  103.3 0.8 copy.137
  104.6 9.6 %all-gather.27 = bf16[4,3,512]{2,1,0:T(4,128)(2,1)S(1)} all-gather(bf16[1,3,512]{2,1,0:T(4,128)(2,1)S(1)} %get-tuple-element.19), channel_id=12, replica_groups=mesh['node_0'=4,'node_1'=2,'node_2'=4,'node_3'=2,'local'=4] {'node_2'}, dimensions={0}, use_global_device_ids=true | all-gather | bytes 15360 | tf_op jit(solution)/shard_map/all_gather | solution.py:20
  114.2 7.2 all-gather.11
  121.4 9.3 %all-gather.12 = bf16[8,4,3,512]{3,1,2,0:T(4,128)(2,1)S(1)} all-gather(bf16[2,4,3,512]{3,1,2,0:T(4,128)(2,1)S(1)} %copy.139), channel_id=14, replica_groups=mesh['node_0'=4,'node_1'=2,'node_2'=4,'node_3'=2,'local'=4] {'node_0'}, dimensions={0}, use_global_device_ids=true | all-gather | bytes 122880 | tf_op jit(solution)/shard_map/all_gather | solution.py:20
  130.7 11.4 %all-gather.13 = bf16[16,2,4,3,512]{4,2,3,1,0:T(4,128)(2,1)S(1)} all-gather(bf16[4,2,4,3,512]{4,2,3,1,0:T(4,128)(2,1)S(1)} %bitcast.156), channel_id=15, replica_groups=mesh['node_0'=4,'node_1'=2,'node_2'=4,'node_3'=2,'local'=4] {'local'}, dimensions={0}, use_global_device_ids=true | all-gather | bytes 491520 | tf_op jit(solution)/shard_map/all_gather | solution.py:20
  142.2 16.9 %all-gather.14 = bf16[8,4,2,4,3,512]{5,3,4,2,1,0:T(4,128)(2,1)S(1)} all-gather(bf16[4,4,2,4,3,512]{5,3,4,2,1,0:T(4,128)(2,1)S(1)} %bitcast.147), channel_id=16, replica_groups=mesh['node_0'=4,'node_1'=2,'node_2'=4,'node_3'=2,'local'=4] {'node_3'}, dimensions={0}, use_global_device_ids=true | all-gather | bytes 1179648 | tf_op jit(solution)/shard_map/all_gather | solution.py:20
  159.1 1.6 copy.175
  160.7 7.1 all-gather.28
  167.8 9.0 %all-gather.16 = bf16[8,3,512]{2,1,0:T(4,128)(2,1)S(1)} all-gather(bf16[2,3,512]{2,1,0:T(4,128)(2,1)S(1)} %all-gather.28), channel_id=18, replica_groups=mesh['node_0'=4,'node_1'=2,'node_2'=4,'node_3'=2,'local'=4] {'node_0'}, dimensions={0}, use_global_device_ids=true | all-gather | bytes 30720 | tf_op jit(solution)/shard_map/all_gather | solution.py:20
  176.8 10.3 %all-gather.17 = bf16[16,2,3,512]{3,1,2,0:T(2,128)(2,1)S(1)} all-gather(bf16[4,2,3,512]{3,1,2,0:T(2,128)(2,1)S(1)} %copy.141), channel_id=19, replica_groups=mesh['node_0'=4,'node_1'=2,'node_2'=4,'node_3'=2,'local'=4] {'local'}, dimensions={0}, use_global_device_ids=true | all-gather | bytes 122880 | tf_op jit(solution)/shard_map/all_gather | solution.py:20
  187.2 8.9 %all-gather.18 = bf16[8,4,2,3,512]{4,1,3,2,0:T(4,128)(2,1)S(1)} all-gather(bf16[4,4,2,3,512]{4,1,3,2,0:T(4,128)(2,1)S(1)} %copy.142), channel_id=20, replica_groups=mesh['node_0'=4,'node_1'=2,'node_2'=4,'node_3'=2,'local'=4] {'node_3'}, dimensions={0}, use_global_device_ids=true | all-gather | bytes 294912 | tf_op jit(solution)/shard_map/all_gather | solution.py:20
  196.1 12.4 %all-gather.19 = bf16[8,4,4,2,3,512]{5,2,4,3,1,0:T(4,128)(2,1)S(1)} all-gather(bf16[2,4,4,2,3,512]{5,2,4,3,1,0:T(4,128)(2,1)S(1)} %bitcast.149), channel_id=21, replica_groups=mesh['node_0'=4,'node_1'=2,'node_2'=4,'node_3'=2,'local'=4] {'node_2'}, dimensions={0}, use_global_device_ids=true | all-gather | bytes 983040 | tf_op jit(solution)/shard_map/all_gather | solution.py:20
  208.4 0.9 copy-done.2
  209.3 1.6 copy.178
  210.9 10.2 %all-gather.25 = bf16[4,3,512]{2,1,0:T(4,128)(2,1)S(1)} all-gather(bf16[1,3,512]{2,1,0:T(4,128)(2,1)S(1)} %get-tuple-element.21), channel_id=2, replica_groups=mesh['node_0'=4,'node_1'=2,'node_2'=4,'node_3'=2,'local'=4] {'local'}, dimensions={0}, use_global_device_ids=true | all-gather | bytes 15360 | tf_op jit(solution)/shard_map/all_gather | solution.py:20
  221.1 6.3 all-gather.1
  227.5 9.8 %all-gather.2 = bf16[8,4,3,512]{3,1,2,0:T(4,128)(2,1)S(1)} all-gather(bf16[2,4,3,512]{3,1,2,0:T(4,128)(2,1)S(1)} %copy.133), channel_id=4, replica_groups=mesh['node_0'=4,'node_1'=2,'node_2'=4,'node_3'=2,'local'=4] {'node_2'}, dimensions={0}, use_global_device_ids=true | all-gather | bytes 122880 | tf_op jit(solution)/shard_map/all_gather | solution.py:20
  237.3 9.2 %all-gather.3 = bf16[8,2,4,3,512]{4,2,3,1,0:T(4,128)(2,1)S(1)} all-gather(bf16[4,2,4,3,512]{4,2,3,1,0:T(4,128)(2,1)S(1)} %bitcast.155), channel_id=5, replica_groups=mesh['node_0'=4,'node_1'=2,'node_2'=4,'node_3'=2,'local'=4] {'node_1'}, dimensions={0}, use_global_device_ids=true | all-gather | bytes 294912 | tf_op jit(solution)/shard_map/all_gather | solution.py:20
  246.5 10.8 %all-gather.4 = bf16[8,4,2,4,3,512]{5,3,4,2,1,0:T(4,128)(2,1)S(1)} all-gather(bf16[2,4,2,4,3,512]{5,3,4,2,1,0:T(4,128)(2,1)S(1)} %bitcast.150), channel_id=6, replica_groups=mesh['node_0'=4,'node_1'=2,'node_2'=4,'node_3'=2,'local'=4] {'node_0'}, dimensions={0}, use_global_device_ids=true | all-gather | bytes 983040 | tf_op jit(solution)/shard_map/all_gather | solution.py:20
  257.3 1.7 copy.134
  259.0 4.1 copy.190
  263.1 3.4 copy.191
  266.5 1.0 reshape.134
  268.2 1.2 broadcast_multiply_fusion
  269.4 6.2 fusion.15
  275.6 2.8 copy.147
  278.4 53.8 %concatenate.23 = bf16[256,16,512]{2,1,0:T(8,128)(2,1)} concatenate(bf16[256,3,512]{2,1,0:T(4,128)(2,1)} %bitcast.123, bf16[256,3,512]{2,1,0:T(4,128)(2,1)S(1)} %bitcast.121, bf16[256,3,512]{2,1,0:T(4,128)(2,1)} %bitcast.135, bf16[256,3,512]{2,1,0:T(4,128)(2,1)} %bitcast.136, bf16[256,4,512]{2,1,0:T(4,128)(2,1)} %bitcast.125), dimensions={1} | concatenate | bytes 8388608 | tf_op jit(solution)/shard_map/concatenate | solution.py:42
  332.2 3.5 fusion.31
  335.7 0.8 fusion.30
  336.5 2.0 copy.188
  338.4 1.1 copy.189
  339.5 1.4 subtract_convert_fusion
  340.9 6.1 fusion.20
  347.0 12.9 %fusion.13 = f32[4,8,256,256]{2,3,1,0:T(8,128)} fusion(f32[4,256,256,8]{2,1,3,0:T(8,128)} %fusion.20, pred[256,256]{0,1:T(8,128)(4,1)} %fusion.24), kind=kOutput, calls=%fused_computation.18 | output fusion | flops 12599806 | bytes 16842752 | tf_op jit(solution)/shard_map/div | solution.py:93
  359.9 14.2 %fusion.17 = f32[256,4,128]{2,0,1:T(8,128)} fusion(bf16[256,4,8,128]{0,3,2,1:T(8,128)(2,1)} %bitcast.130, f32[4,8,256,256]{2,3,1,0:T(8,128)} %fusion.13, f32[4,256,256,8]{2,1,3,0:T(8,128)} %fusion.15), kind=kOutput, calls=%fused_computation.22 | convolution fusion | flops 547365120 | bytes 19398656 | tf_op jit(solution)/shard_map/kgts,tkgd->skd/dot_general | solution.py:99
  374.1 1.6 multiply_subtract_fusion
  375.7 0.9 maximum_convert_fusion
  376.5 1.1 copy.159
  377.6 4.5 convolution_bitcast_fusion
  382.1 9.0 %copy.183 = f32[4096,512]{1,0:T(8,128)} copy(f32[4096,512]{0,1:T(8,128)} %convolution_bitcast_fusion) | data formatting | bytes 16777216
  391.1 1.7 copy.162
  392.9 1.5 copy.164
  394.4 1.5 copy.145
  396.0 1.6 copy.165
  397.6 53.8 %concatenate.31 = bf16[64,4,16,512]{3,2,1,0:T(8,128)(2,1)} concatenate(bf16[64,4,3,512]{3,2,1,0:T(4,128)(2,1)} %bitcast.124, bf16[64,4,3,512]{3,2,1,0:T(4,128)(2,1)S(1)} %bitcast.122, bf16[64,4,3,512]{3,2,1,0:T(4,128)(2,1)} %copy.164, bf16[64,4,3,512]{3,2,1,0:T(4,128)(2,1)} %copy.165, bf16[64,4,4,512]{3,2,1,0:T(4,128)(2,1)} %bitcast.126), dimensions={2} | concatenate | bytes 8388608 | tf_op jit(solution)/shard_map/concatenate | solution.py:42
  451.4 1.3 constant_dynamic-slice_fusion
  453.1 118.3 %all_to_all.10 = bf16[4,1024,512]{2,1,0:T(8,128)(2,1)} all-to-all(bf16[4,1024,512]{2,1,0:T(8,128)(2,1)S(1)} %stack.3), channel_id=1, replica_groups=mesh['node_0'=4,'node_1'=2,'node_2'=4,'node_3'=2,'local'=4] {'local'}, dimensions={0} | all-to-all | bytes 8388608 | tf_op jit(solution)/shard_map/all_to_all | solution.py:124
  571.4 249.6 %reduce-scatter.4.cloned.1.call-done = f32[64,512]{1,0:T(8,128)} async-done(((f32[4096,512]{1,0:T(8,128)}), f32[64,512]{1,0:T(8,128)}) %reduce-scatter.4.cloned.1.call-update) | async-done | bytes 131088 | tf_op jit(solution)/shard_map/reduce_scatter | solution.py:131
  821.0 7.2 all-to-all-start.1
  828.2 4.8 convolution_convert_fusion
  833.0 4.1 copy.166
  837.1 3.2 copy.167
  840.3 4.1 copy.169
  (25 shorter events, 2.5 us)
Async XLA Ops:
  7.2 325.0 %copy-start = (bf16[256,4096]{1,0:T(8,128)(2,1)S(1)}, bf16[256,4096]{1,0:T(8,128)(2,1)}, u32[]{:S(2)}) copy-start(bf16[256,4096]{1,0:T(8,128)(2,1)} %param.6) | copy-start | bytes 6291460
  7.2 268.4 %all-gather.32.cloned.1.call-start = ((), (), s32[]{:S(2)}) async-start(), calls=%async_computation.3 | async-start | bytes 1572864 | tf_op jit(solution)/shard_map/all_gather | solution.py:20
  49.0 772.0 %reduce-scatter.4.cloned.1.call-start = ((), (), s32[]{:S(2)}) async-start(), calls=%async_computation.4 | async-start | bytes 8519680 | tf_op jit(solution)/shard_map/reduce_scatter | solution.py:131
  159.1 99.9 %copy-start.1 = (bf16[8,4,2,4,3,512]{5,3,4,2,1,0:T(4,128)(2,1)}, bf16[8,4,2,4,3,512]{5,3,4,2,1,0:T(4,128)(2,1)S(1)}, u32[]{:S(2)}) copy-start(bf16[8,4,2,4,3,512]{5,3,4,2,1,0:T(4,128)(2,1)S(1)} %all-gather.14) | copy-start | bytes 2359300
  159.1 99.9 %copy-start.3 = (s32[256]{0:T(256)S(1)}, s32[256]{0:T(256)}, u32[]{:S(2)}) copy-start(s32[256]{0:T(256)} %param.11) | copy-start | bytes 3076
  208.4 0.9 copy-start.2
  821.0 23.4 %all-to-all-start.1 = ((f32[4,16,512]{2,1,0:T(8,128)}), f32[4,16,512]{2,1,0:T(8,128)S(1)}, u32[]{:S(2)}, u32[]{:S(2)}) async-start(f32[4,16,512]{2,1,0:T(8,128)} %bitcast.163), calls=%async_computation.1 | async-start | bytes 262144 | tf_op jit(solution)/shard_map/all_to_all | solution.py:53
Sparse Core Ops, SparseCore 0:
  49.1 42.8 all-gather.31
  391.3 429.7 reduce-scatter.3
